TPU v7x, 128 devices: a whole 4x4x4 slice. The times are simulated.
128 devices in a mesh: dp: 4 (over z_hi, core), fsdp: 32 (over z_lo, y, x).
Axes of the slice: x: 4, y: 4, z: 4 (z_hi: 2, z_lo: 2; z = z_hi * 2 + z_lo), core: 2. Of those that a mesh axis runs over, the one named last changes fastest.
Arguments:
- grad_partial: float32 [4, 160, 512, 512], P('dp', None, 'fsdp'), may hold values from -6 to 6
- params: bfloat16 [160, 512, 512], P(None, 'fsdp'), may hold values from -0.75 to 0.75
- stats_left: float32 [256, 512, 512], P(('dp', 'fsdp')), as said below
- stats_right: float32 [256, 512, 512], P(('dp', 'fsdp')), as said below
- roots_left: float32 [256, 512, 512], P(('dp', 'fsdp')), as said below
- roots_right: float32 [256, 512, 512], P(('dp', 'fsdp')), as said below
- owner: int32 [160], replicated, may hold values from 0 to 127, as said below
- refresh: int32 [160], replicated, may hold values from 0 to 1, as said below
Outputs:
- new_params: bfloat16 [160, 512, 512], P(None, 'fsdp')
- new_left: float32 [256, 512, 512], P(('dp', 'fsdp'))
- new_right: float32 [256, 512, 512], P(('dp', 'fsdp'))
Inputs may be any that keep to these rules, and one draw needn't show every extreme that they name: owner[b] is the index (dp index times 32 plus fsdp index) of the device that owns block b; every device owns one or two blocks, none more than 2. refresh is 1 on exactly 20 blocks, each owned by a device that owns no other block, and 0 elsewhere; the device whose fsdp index differs from such an owner's in the lowest bit owns no block with refresh 1. `stats_left`: symmetric positive definite, smallest eigenvalue 0.05 or more. `stats_right`: symmetric positive definite, smallest eigenvalue 0.05 or more. `roots_left`: symmetric positive definite. `roots_right`: symmetric positive definite.
All inputs are finite; a program needn't handle non-finite values.
Results may differ from a plain program's by a relative error of at most 0.0051.
Values may be sent and summed in bfloat16 or wider, within the bound.
A program may use at most 128 MiB of HBM per device.

v0:
```python
import jax
import jax.numpy as jnp
from jax import lax
from jax.experimental import pallas as pl
from jax.experimental.pallas import tpu as pltpu
from jax.sharding import PartitionSpec as P

MESH = pl.DeviceIdType.MESH
F32 = jnp.float32
BF16 = jnp.bfloat16

beta_decay = 0.9
learn_rate = 0.2
epsilon = 1e-06
ITERS = 6

PLANES = 4
SIDE = 4
COLS = SIDE * SIDE
CORES = 2
CAP = 2
ROWS = 16
WIDTH = 512
SLOTS = CORES * PLANES * CAP * COLS
HOPS = (1, 3, 2)
CHUNKS = HOPS + (0,)
AHEAD, BEHIND, SECOND = range(3)
PARTS = ((0, 0, COLS // 2, 2), (0, COLS // 2, COLS // 2, 2), (1, 0, COLS, 1))


class Place:
    def __init__(self):
        dp = lax.axis_index("dp")
        fsdp = lax.axis_index("fsdp")
        self.core = lax.rem(dp, 2)
        self.plane = (dp // 2) * 2 + fsdp // COLS
        self.low = fsdp // COLS
        self.col = lax.rem(fsdp, COLS)

    def at(self, core, plane, col):
        return ((plane // 2) * 2 + core, lax.rem(plane, 2) * COLS + col)

    def sibling(self):
        return self.at(1 - self.core, self.plane, self.col)

    def up(self, hop):
        return lax.rem(self.plane + hop, PLANES)

    def above(self, hop):
        return self.at(self.core, self.up(hop), self.col)

    def turn(self, t):
        y, x = self.col // SIDE, lax.rem(self.col, SIDE)
        return lax.rem(y + t // SIDE, SIDE) * SIDE + lax.rem(x + lax.rem(t, SIDE), SIDE)

    def half(self, which):
        return 1 - self.low if which == 0 else self.low


def greet(place):
    partners = [place.sibling()] + [place.above(hop) for hop in HOPS]
    partners += [place.at(place.core, place.plane, place.turn(t)) for t in range(1, COLS)]
    for partner in partners:
        pl.semaphore_signal(pltpu.get_barrier_semaphore(), inc=1, device_id=partner, device_id_type=MESH)
    return len(partners)


def spread_order(i):
    return lax.rem(5 * i, COLS)


def count_up(mask, axis):
    return jnp.sum(mask.astype(jnp.int32), axis=axis, keepdims=True)


def index_tables(owner, refresh, device):
    count = owner.shape[1]
    row = lax.broadcasted_iota(jnp.int32, (count, count), 0)
    column = lax.broadcasted_iota(jnp.int32, (count, count), 1)
    owner_down = jnp.sum(jnp.where(row == column, owner, 0), axis=1, keepdims=True)
    refresh_down = jnp.sum(jnp.where(row == column, refresh, 0), axis=1, keepdims=True)
    same = owner_down == owner
    other_down = count_up(((owner_down ^ 1) == owner) & (refresh > 0), 1)
    ahead_down = (refresh_down > 0) | (((owner_down & 1) == 0) & (other_down == 0))
    rank = count_up(same & (row < column), 0)
    rank_down = count_up(same & (column < row), 1)

    def first(own):
        core, plane = (own >> 5) & 1, 2 * (own >> 6) + ((own >> 4) & 1)
        return (core * PLANES + plane) * CAP * COLS

    entry = first(owner) + (rank + refresh) * COLS + (owner & (COLS - 1))
    col_down = owner_down & (COLS - 1)
    pair_down = (col_down >> 1) + jnp.where(ahead_down, 0, COLS // 2)
    place_down = first(owner_down) + jnp.where(rank_down > 0, COLS + col_down, pair_down)
    spot = lax.broadcasted_iota(jnp.int32, (count, SLOTS), 1)
    block = lax.broadcasted_iota(jnp.int32, (count, SLOTS), 0)
    packed = jnp.sum(jnp.where(place_down == spot, block, 0), axis=0, keepdims=True)
    mine = owner == device
    live = [count_up(mine & (rank == slot), 1) for slot in range(CAP)]
    fresh = count_up(mine & (refresh > 0), 1)
    other = count_up((owner == (device ^ 1)) & (refresh > 0), 1)
    ahead = (fresh > 0) | (((device & 1) == 0) & (other == 0))
    return jnp.minimum(packed, count - 1), jnp.minimum(entry, SLOTS - 1), live, fresh, ahead


def remote(src, dst, send, recv, device):
    return pltpu.make_async_remote_copy(
        src_ref=src, dst_ref=dst, send_sem=send, recv_sem=recv, device_id=device, device_id_type=MESH
    )


def dot(left, right):
    return jnp.dot(left, right, preferred_element_type=F32)


def dot_t(left, right, dims):
    return lax.dot_general(left, right, ((dims, dims), ((), ())), preferred_element_type=F32)


def halves(value):
    high = value.astype(BF16)
    return high, (value - high.astype(F32)).astype(BF16)


def total_square(value):
    return jnp.sum(value * value, axis=(0, 1), keepdims=True)


def root_start(factor, result, mixed):
    scale = jnp.sqrt(total_square(factor) + epsilon)
    start = factor / scale
    mixed[...] = start
    row = lax.broadcasted_iota(jnp.int32, start.shape, 0)
    column = lax.broadcasted_iota(jnp.int32, start.shape, 1)
    ident = jnp.where(row == column, 1.0, 0.0).astype(F32)
    result[...] = lax.rsqrt(jnp.sqrt(scale)) * (1.25 * ident - 0.25 * start)


def root_sweep(result, mixed):
    now = mixed[...]
    low = now.astype(BF16)
    edge = (dot(low, low) - 10.0 * now) * (1.0 / 16.0)
    edge_low = edge.astype(BF16)
    fourth = dot(edge_low, edge_low) + 3.125 * edge
    now = (625.0 / 256.0) * now + dot(fourth.astype(BF16), low)
    mixed[...] = now
    held = result[...]
    result[...] = 1.25 * held - 0.25 * dot(held.astype(BF16), now.astype(BF16))


def scaled_step(precond, grad):
    ratio = jnp.sqrt(total_square(grad.astype(F32))) / jnp.sqrt(total_square(precond) + epsilon)
    return (learn_rate * precond * ratio).astype(BF16)


def kept_step(inv_left, grad, inv_right):
    left_high, left_low = halves(inv_left)
    inner_high, inner_low = halves(dot(left_high, grad) + dot(left_low, grad))
    right_high, right_low = halves(inv_right)
    precond = dot(inner_high, right_high) + (dot(inner_low, right_high) + dot(inner_high, right_low))
    return scaled_step(precond, grad)


def whole_kernel(
    owner_hbm, refresh_hbm, grad_hbm, params_hbm, stats_left, stats_right, roots_left, roots_right,
    result_ref, gram,
    owner_ref, refresh_ref, table_vmem, table, grad_ref, keep, inverse, mixed,
    core_out, core_in, plane_out, plane_in, col_out, held, step, rows, every,
    local_sems, core_s, core_r, plane_s, plane_r, col_s, col_r,
    row_s, row_r, up_s, up_r, back_s, back_r, core_s2, core_r2,
):
    place = Place()
    loads = [
        pltpu.make_async_copy(owner_hbm, owner_ref, local_sems.at[7]),
        pltpu.make_async_copy(refresh_hbm, refresh_ref, local_sems.at[8]),
        pltpu.make_async_copy(grad_hbm.at[0], grad_ref, local_sems.at[0]),
    ]
    for copy in loads:
        copy.start()
    partners = greet(place)
    device = lax.axis_index("dp") * lax.axis_size("fsdp") + lax.axis_index("fsdp")
    loads[0].wait()
    loads[1].wait()
    packed, entry, live, fresh, ahead = index_tables(owner_ref[...], refresh_ref[...], device)
    table_vmem[0:1, :] = packed
    table_vmem[1:2, 0 : entry.shape[1]] = entry
    load_table = pltpu.make_async_copy(table_vmem, table, local_sems.at[6])
    load_table.start()
    pl.semaphore_wait(pltpu.get_barrier_semaphore(), partners)
    load_table.wait()
    loads[2].wait()

    def base(core, hop, part):
        slot, at, _, _ = PARTS[part]
        return ((core * PLANES + place.up(hop)) * CAP + slot) * COLS + at

    core_copies = {}
    plane_copies = {}

    def pack(part):
        slot, at, size, _ = PARTS[part]
        for h, hop in enumerate(CHUNKS):
            start = base(1 - place.core, hop, part)
            if part == SECOND:
                core_copies[AHEAD, h].wait_send()
                core_copies[BEHIND, h].wait_send()

            def one(e, carry, h=h, start=start):
                core_out[h, at + e] = grad_ref[table[0, start + e]]
                return carry

            lax.fori_loop(0, size, one, 0, unroll=4)
            span = pl.ds(at, size)
            core_copies[part, h] = remote(
                core_out.at[h, span], core_in.at[slot, h, span], core_s.at[part, h], core_r.at[part, h], place.sibling()
            )
            core_copies[part, h].start()

    def add(part):
        slot, at, size, _ = PARTS[part]
        for h, hop in enumerate(CHUNKS):
            core_copies[part, h].wait_recv()
            start = base(place.core, hop, part)

            def one(e, carry, h=h, hop=hop, start=start):
                total = grad_ref[table[0, start + e]] + core_in[slot, h, at + e]
                if hop:
                    plane_out[slot, h, at + e] = total.astype(BF16)
                else:
                    core_in[slot, h, at + e] = total
                return carry

            lax.fori_loop(0, size, one, 0, unroll=4)
            if hop:
                span = pl.ds(at, size)
                plane_copies[part, h] = remote(
                    plane_out.at[slot, h, span], plane_in.at[slot, h, span], plane_s.at[part, h], plane_r.at[part, h],
                    place.above(hop),
                )
                if part != SECOND:
                    plane_copies[part, h].start()

    def planes_send(part):
        for h in range(len(HOPS)):
            plane_copies[part, h].start()

    def col_copy(part, which, t):
        slot, at, _, share = PARTS[part]
        col, half = place.turn(t), place.half(which)
        return remote(
            col_out.at[slot, half, at + col // share], held.at[part, half, place.col],
            col_s.at[part, which, t], col_r.at[part, which, t], place.at(place.core, place.plane, col),
        )

    def fold(part, which):
        slot, at, size, share = PARTS[part]
        half = place.half(which)
        for h, hop in enumerate(HOPS):
            if (hop == 2) == (which == 1):
                plane_copies[part, h].wait_recv()

        def one(e, carry):
            if which == 0:
                total = plane_in[slot, 0, at + e].astype(F32) + plane_in[slot, 1, at + e].astype(F32)
            else:
                total = core_in[slot, len(HOPS), at + e] + plane_in[slot, 2, at + e].astype(F32)
            col_out[slot, half, at + e] = total.astype(BF16)
            return carry

        lax.fori_loop(0, size, one, 0, unroll=4)

        def send(i, carry):
            col_copy(part, which, spread_order(i)).start()
            return carry

        lax.fori_loop(1, COLS, send, 0)
        held[part, half, place.col] = col_out[slot, half, at + place.col // share]

    def col_wait(part):
        for which in range(2):

            def one(t, carry):
                col_copy(part, which, t).wait_recv()
                return carry

            lax.fori_loop(1, COLS, one, 0)

    def region(plane, slot):
        return ((place.core * PLANES + plane) * CAP + slot) * COLS

    def row_copy(which, t):
        col, half = place.turn(t), place.half(which)
        return remote(
            step.at[0, half, col], rows.at[half, place.col],
            row_s.at[which, t], row_r.at[which, t], place.at(place.core, place.plane, col),
        )

    def rows_send():
        for which in range(2):

            def one(i, carry):
                row_copy(which, spread_order(i)).start()
                return carry

            lax.fori_loop(1, COLS, one, 0)
        rows[:, place.col] = step[0, :, place.col]

    up_copies = {}

    def rows_up():
        for which in range(2):

            def one(t, carry):
                row_copy(which, t).wait_recv()
                return carry

            lax.fori_loop(1, COLS, one, 0)
            for h, hop in enumerate(HOPS):
                if (hop == 2) == (which == 1):
                    up_copies[h] = remote(
                        rows.at[place.half(which)], every.at[pl.ds(region(place.plane, 0), COLS)],
                        up_s.at[h], up_r.at[h], place.above(hop),
                    )
                    up_copies[h].start()
        every[pl.ds(region(place.plane, 0), COLS)] = rows[place.low]

    def back_copy(h, t):
        plane, col = place.up(CHUNKS[h]), place.turn(t)
        return remote(
            step.at[1, lax.rem(plane, 2), col], every.at[region(place.plane, 1) + place.col],
            back_s.at[h, t], back_r.at[h, t], place.at(place.core, plane, col),
        )

    def back_send():
        def far(i, carry):
            back_copy(2, spread_order(i)).start()
            return carry

        def near(i, carry):
            back_copy(0, spread_order(i)).start()
            back_copy(1, spread_order(i)).start()
            return carry

        def here(i, carry):
            back_copy(3, spread_order(i)).start()
            return carry

        lax.fori_loop(0, COLS, far, 0)
        lax.fori_loop(0, COLS, near, 0)
        lax.fori_loop(1, COLS, here, 0)
        every[region(place.plane, 1) + place.col] = step[1, place.low, place.col]

    def back_wait(h):
        def one(t, carry):
            back_copy(h, t).wait_recv()
            return carry

        lax.fori_loop(int(CHUNKS[h] == 0), COLS, one, 0)

    back_cores = {}

    def over(slot, h):
        here = every.at[pl.ds(region(place.up(PLANES - CHUNKS[h]), slot), COLS)]
        back_cores[slot, h] = remote(here, here, core_s2.at[slot, h], core_r2.at[slot, h], place.sibling())
        back_cores[slot, h].start()

    pack(AHEAD)
    pack(BEHIND)
    add(AHEAD)
    loads = []
    for i, (src, dst) in enumerate(
        ((stats_left, gram.at[0]), (stats_right, gram.at[1]), (roots_left, keep.at[0]), (roots_right, keep.at[1]),
         (params_hbm, result_ref))
    ):
        copy = pltpu.make_async_copy(src, dst, local_sems.at[1 + i])
        copy.start()
        loads.append(copy)
    add(BEHIND)
    pack(SECOND)
    fold(AHEAD, 0)
    fold(AHEAD, 1)
    add(SECOND)
    fold(BEHIND, 0)
    planes_send(SECOND)
    fold(BEHIND, 1)
    for copy in loads:
        copy.wait()

    def grad_of(part):
        return held[part].reshape(WIDTH, WIDTH)

    def first_grad():
        both = jnp.where(ahead, grad_of(AHEAD).astype(F32), grad_of(BEHIND).astype(F32))
        return both.astype(BF16)

    def put_step(slot, value):
        step[slot] = value.reshape(2, COLS, ROWS, WIDTH)

    def factor(side, slot, grad):
        fresh_part = dot_t(grad, grad, ((1,), (0,))[side])
        return beta_decay * gram[side, slot] + ((1.0 - beta_decay) / WIDTH) * fresh_part

    def factors(slot, grad):
        for side in range(2):
            gram[side, slot] = live[slot].astype(F32) * factor(side, slot, grad)

    def sweeps(count):
        def one(i, carry):
            root_sweep(inverse.at[0], mixed.at[0])
            root_sweep(inverse.at[1], mixed.at[1])
            return carry

        lax.fori_loop(0, count, one, 0)

    col_wait(AHEAD)
    for side in range(2):
        root_start(factor(side, 0, grad_of(AHEAD)), inverse.at[side], mixed.at[side])
    sweeps(1)
    col_wait(BEHIND)
    put_step(0, kept_step(keep[0, 0], first_grad(), keep[1, 0]))
    rows_send()
    sweeps(1)
    fold(SECOND, 0)
    fold(SECOND, 1)
    sweeps(1)
    rows_up()
    sweeps(2)
    col_wait(SECOND)
    put_step(1, kept_step(keep[0, 1], grad_of(SECOND), keep[1, 1]))
    grad = grad_of(AHEAD)
    inner = dot(inverse[0].astype(BF16), grad)
    renewed = scaled_step(dot(inner.astype(BF16), inverse[1].astype(BF16)), grad)
    late = step[1].reshape(WIDTH, WIDTH)
    put_step(1, jnp.where(fresh > 0, renewed.astype(F32), late.astype(F32)).astype(BF16))
    back_send()
    factors(0, first_grad())
    factors(1, grad_of(SECOND))
    over(0, 3)
    for h in range(len(HOPS)):
        up_copies[h].wait_recv()
        over(0, h)
    for h in range(PLANES):
        core_copies[SECOND, h].wait_send()
    for copy in plane_copies.values():
        copy.wait_send()
    for part in range(len(PARTS)):
        for which in range(2):

            def done(t, carry):
                col_copy(part, which, t).wait_send()
                return carry

            lax.fori_loop(1, COLS, done, 0)
    for which in range(2):

        def row_done(t, carry):
            row_copy(which, t).wait_send()
            return carry

        lax.fori_loop(1, COLS, row_done, 0)
    for copy in up_copies.values():
        copy.wait_send()
    for h in (2, 0, 1, 3):
        back_wait(h)
        over(1, h)
    for h in range(len(CHUNKS)):

        def back_done(t, carry):
            back_copy(h, t).wait_send()
            return carry

        lax.fori_loop(int(CHUNKS[h] == 0), COLS, back_done, 0)
    for copy in back_cores.values():
        copy.wait_recv()

    def apply(b, carry):
        change = every[table[1, b]].astype(F32)
        result_ref[b] = (result_ref[b].astype(F32) - change).astype(BF16)
        return carry

    lax.fori_loop(0, result_ref.shape[0], apply, 0, unroll=4)
    for copy in back_cores.values():
        copy.wait_send()


def store_kernel(result_ref, gram, out_params, out_left, out_right, sems):
    copies = [
        pltpu.make_async_copy(gram.at[0], out_left, sems.at[0]),
        pltpu.make_async_copy(gram.at[1], out_right, sems.at[1]),
        pltpu.make_async_copy(result_ref, out_params, sems.at[2]),
    ]
    for copy in copies:
        copy.start()
    for copy in copies:
        copy.wait()


VMEM = pl.BlockSpec(memory_space=pltpu.VMEM)
HBM = pl.BlockSpec(memory_space=pltpu.HBM)


def body(grad_partial, params, stats_left, stats_right, roots_left, roots_right, owner, refresh):
    count = params.shape[0]
    dma = pltpu.SemaphoreType.DMA
    hops = len(HOPS)
    piece = (COLS, ROWS, WIDTH)
    square = (WIDTH, WIDTH)
    result, gram = pl.pallas_call(
        whole_kernel,
        name="whole",
        out_shape=[pltpu.VMEM(params.shape, BF16), pltpu.VMEM((2, CAP) + square, F32)],
        in_specs=[HBM] * 8,
        out_specs=[VMEM] * 2,
        scratch_shapes=[
            pltpu.VMEM((1, count), jnp.int32),
            pltpu.VMEM((1, count), jnp.int32),
            pltpu.VMEM((8, SLOTS), jnp.int32),
            pltpu.SMEM((8, SLOTS), jnp.int32),
            pltpu.VMEM((count, ROWS, WIDTH), F32),
            pltpu.VMEM((2, CAP) + square, F32),
            pltpu.VMEM((2,) + square, F32),
            pltpu.VMEM((2,) + square, F32),
            pltpu.VMEM((PLANES,) + piece, F32),
            pltpu.VMEM((CAP, PLANES) + piece, F32),
            pltpu.VMEM((CAP, hops) + piece, BF16),
            pltpu.VMEM((CAP, hops) + piece, BF16),
            pltpu.VMEM((CAP, 2) + piece, BF16),
            pltpu.VMEM((len(PARTS), 2) + piece, BF16),
            pltpu.VMEM((CAP, 2) + piece, BF16),
            pltpu.VMEM((2,) + piece, BF16),
            pltpu.VMEM((SLOTS, ROWS, WIDTH), BF16),
            dma((9,)),
            dma((len(PARTS), PLANES)), dma((len(PARTS), PLANES)),
            dma((len(PARTS), hops)), dma((len(PARTS), hops)),
            dma((len(PARTS), 2, COLS)), dma((len(PARTS), 2, COLS)),
            dma((2, COLS)), dma((2, COLS)),
            dma((hops,)), dma((hops,)),
            dma((PLANES, COLS)), dma((PLANES, COLS)),
            dma((CAP, PLANES)), dma((CAP, PLANES)),
        ],
        compiler_params=pltpu.CompilerParams(collective_id=0, has_side_effects=True, vmem_limit_bytes=40 << 20),
    )(*[
        pltpu.with_memory_space_constraint(array, pltpu.HBM)
        for array in (
            owner.reshape(1, count), refresh.reshape(1, count),
            grad_partial, params, stats_left, stats_right, roots_left, roots_right,
        )
    ])
    return pl.pallas_call(
        store_kernel,
        name="store",
        out_shape=[
            jax.ShapeDtypeStruct(params.shape, BF16),
            jax.ShapeDtypeStruct((CAP,) + square, F32),
            jax.ShapeDtypeStruct((CAP,) + square, F32),
        ],
        in_specs=[VMEM] * 2,
        out_specs=[HBM] * 3,
        scratch_shapes=[dma((3,))],
        compiler_params=pltpu.CompilerParams(vmem_limit_bytes=1 << 20),
    )(
        pltpu.with_memory_space_constraint(result, pltpu.VMEM),
        pltpu.with_memory_space_constraint(gram, pltpu.VMEM),
    )


def solution(mesh):
    in_specs = (
        P("dp", None, "fsdp", None),
        P(None, "fsdp", None),
        P(("dp", "fsdp"), None, None),
        P(("dp", "fsdp"), None, None),
        P(("dp", "fsdp"), None, None),
        P(("dp", "fsdp"), None, None),
        P(),
        P(),
    )
    out_specs = (
        P(None, "fsdp", None),
        P(("dp", "fsdp"), None, None),
        P(("dp", "fsdp"), None, None),
    )
    return jax.shard_map(body, mesh=mesh, in_specs=in_specs, out_specs=out_specs, check_vma=False)
```

profile of v0, /device:TPU:1, one launch (start us, length us, event | category | flops | bytes accessed | tf_op | source)
XLA Modules:
  0.0 77.5 jit_solution(9933625757516002934)
XLA Ops:
  0.6 73.8 %whole.1 = (bf16[160,16,512]{2,1,0:T(8,128)(2,1)S(1)}, f32[2,2,512,512]{3,2,1,0:T(8,128)S(1)}) custom-call(s32[1,160]{1,0:T(1,128)} %bitcast.2, s32[1,160]{1,0:T(1,128)} %bitcast.3, f32[1,160,16,512]{3,2,1,0:T(8,128)} %grad_hbm.1, bf16[160,16,512]{2,1,0:T(8,128)(2,1)} %params_hbm.1, f32[2,512,512]{2,1,0:T(8,128)} %stats_left.1, f32[2,512,512]{2,1,0:T(8,128)} %stats_right.1, ...), custom_call_target="tpu_custom_call" | custom-call | tf_op jit(solution)/shard_map/whole/pallas_call | solution.py:509
  74.4 2.9 %store.1 = (bf16[160,16,512]{2,1,0:T(8,128)(2,1)}, f32[2,512,512]{2,1,0:T(8,128)}, f32[2,512,512]{2,1,0:T(8,128)}) custom-call(bf16[160,16,512]{2,1,0:T(8,128)(2,1)S(1)} %get-tuple-element.5.result_ref, f32[2,2,512,512]{3,2,1,0:T(8,128)S(1)} %get-tuple-element.6.gram), custom_call_target="tpu_custom_call" | custom-call | tf_op jit(solution)/shard_map/store/pallas_call | solution.py:550
where the time goes:
time: 77.6 us; the launch traced here: 77.5 us
  Pallas kernels  76.7 us (99%)
  between operations  0.8 us (1%)
    pallas_call x1, Pallas kernels, body(): pl.pallas_call(whole_kernel, name='whole', out_shape=[pltpu.VMEM(params.s...  73.8 us
    pallas_call x1, Pallas kernels, body(): pl.pallas_call(store_kernel, name='store', out_shape=[jax.ShapeDtypeStruc...  2.9 us

commit v1 on v0

--- a/solution.py
+++ b/solution.py
@@ -52,6 +52,10 @@
     def turn(self, t):
         y, x = self.col // SIDE, lax.rem(self.col, SIDE)
         return lax.rem(y + t // SIDE, SIDE) * SIDE + lax.rem(x + lax.rem(t, SIDE), SIDE)
+
+    def turned(self, t):
+        y, x = self.col // SIDE, lax.rem(self.col, SIDE)
+        return lax.rem(y + SIDE - t // SIDE, SIDE) * SIDE + lax.rem(x + SIDE - lax.rem(t, SIDE), SIDE)
 
     def half(self, which):
         return 1 - self.low if which == 0 else self.low
@@ -127,26 +131,39 @@
     return jnp.sum(value * value, axis=(0, 1), keepdims=True)
 
 
-def root_start(factor, result, mixed):
+def root_start(factor, result, mixed, pair):
     scale = jnp.sqrt(total_square(factor) + epsilon)
-    start = factor / scale
+    start = factor * (1.0 / scale)
     mixed[...] = start
     row = lax.broadcasted_iota(jnp.int32, start.shape, 0)
     column = lax.broadcasted_iota(jnp.int32, start.shape, 1)
     ident = jnp.where(row == column, 1.0, 0.0).astype(F32)
-    result[...] = lax.rsqrt(jnp.sqrt(scale)) * (1.25 * ident - 0.25 * start)
-
-
-def root_sweep(result, mixed):
-    now = mixed[...]
-    low = now.astype(BF16)
-    edge = (dot(low, low) - 10.0 * now) * (1.0 / 16.0)
-    edge_low = edge.astype(BF16)
-    fourth = dot(edge_low, edge_low) + 3.125 * edge
-    now = (625.0 / 256.0) * now + dot(fourth.astype(BF16), low)
-    mixed[...] = now
-    held = result[...]
-    result[...] = 1.25 * held - 0.25 * dot(held.astype(BF16), now.astype(BF16))
+    first = lax.rsqrt(jnp.sqrt(scale)) * (1.25 * ident - 0.25 * start)
+    result[...] = first
+    pair[0:WIDTH] = start.astype(BF16)
+    pair[WIDTH : 2 * WIDTH] = first.astype(BF16)
+
+
+def root_sweep(results, mixeds, pairs, with_result):
+    sides = range(len(results))
+    lows = [pair[0:WIDTH] for pair in pairs]
+    products = [dot(pairs[i][...] if with_result else lows[i], lows[i]) for i in sides]
+    edges = [(products[i][0:WIDTH] - 10.0 * mixeds[i][...]) * (1.0 / 16.0) for i in sides]
+    edge_lows = [edge.astype(BF16) for edge in edges]
+    fourths = [dot(edge_lows[i], edge_lows[i]) + 3.125 * edges[i] for i in sides]
+    if with_result:
+        for i in sides:
+            value = 1.25 * results[i][...] - 0.25 * products[i][WIDTH : 2 * WIDTH]
+            results[i][...] = value
+            pairs[i][WIDTH : 2 * WIDTH] = value.astype(BF16)
+    for i in sides:
+        value = (625.0 / 256.0) * mixeds[i][...] + dot(fourths[i].astype(BF16), lows[i])
+        mixeds[i][...] = value
+        pairs[i][0:WIDTH] = value.astype(BF16)
+
+
+def root_end(result, pair):
+    return 1.25 * result[...] - 0.25 * dot(pair[WIDTH : 2 * WIDTH], pair[0:WIDTH])
 
 
 def scaled_step(precond, grad):
@@ -154,10 +171,10 @@
     return (learn_rate * precond * ratio).astype(BF16)
 
 
-def kept_step(inv_left, grad, inv_right):
-    left_high, left_low = halves(inv_left)
-    inner_high, inner_low = halves(dot(left_high, grad) + dot(left_low, grad))
-    right_high, right_low = halves(inv_right)
+def kept_step(left, grad, right):
+    inner = dot(left, grad)
+    inner_high, inner_low = halves(inner[0:WIDTH] + inner[WIDTH : 2 * WIDTH])
+    right_high, right_low = right[0:WIDTH], right[WIDTH : 2 * WIDTH]
     precond = dot(inner_high, right_high) + (dot(inner_low, right_high) + dot(inner_high, right_low))
     return scaled_step(precond, grad)
 
@@ -165,7 +182,7 @@
 def whole_kernel(
     owner_hbm, refresh_hbm, grad_hbm, params_hbm, stats_left, stats_right, roots_left, roots_right,
     result_ref, gram,
-    owner_ref, refresh_ref, table_vmem, table, grad_ref, keep, inverse, mixed,
+    owner_ref, refresh_ref, table_vmem, table, grad_ref, keep, split, inverse, mixed, pair,
     core_out, core_in, plane_out, plane_in, col_out, held, step, rows, every,
     local_sems, core_s, core_r, plane_s, plane_r, col_s, col_r,
     row_s, row_r, up_s, up_r, back_s, back_r, core_s2, core_r2,
@@ -250,8 +267,14 @@
         col, half = place.turn(t), place.half(which)
         return remote(
             col_out.at[slot, half, at + col // share], held.at[part, half, place.col],
-            col_s.at[part, which, t], col_r.at[part, which, t], place.at(place.core, place.plane, col),
+            col_s.at[part, which], col_r.at[part, which], place.at(place.core, place.plane, col),
         )
+
+    def most(ref, send, recv):
+        return remote(ref, ref, send, recv, place.sibling())
+
+    def col_all(part, which):
+        return most(held.at[part, place.half(which), pl.ds(0, COLS - 1)], col_s.at[part, which], col_r.at[part, which])
 
     def fold(part, which):
         slot, at, size, share = PARTS[part]
@@ -279,84 +302,91 @@
 
     def col_wait(part):
         for which in range(2):
-
-            def one(t, carry):
-                col_copy(part, which, t).wait_recv()
-                return carry
-
-            lax.fori_loop(1, COLS, one, 0)
+            col_all(part, which).wait_recv()
 
     def region(plane, slot):
         return ((place.core * PLANES + plane) * CAP + slot) * COLS
 
-    def row_copy(which, t):
-        col, half = place.turn(t), place.half(which)
+    def row_copy(slot, t):
+        col = place.turn(t)
         return remote(
-            step.at[0, half, col], rows.at[half, place.col],
-            row_s.at[which, t], row_r.at[which, t], place.at(place.core, place.plane, col),
+            step.at[slot, 1 - place.low, col], rows.at[slot, place.col],
+            row_s.at[slot], row_r.at[slot, t], place.at(place.core, place.plane, col),
         )
 
-    def rows_send():
-        for which in range(2):
-
-            def one(i, carry):
-                row_copy(which, spread_order(i)).start()
-                return carry
-
-            lax.fori_loop(1, COLS, one, 0)
-        rows[:, place.col] = step[0, :, place.col]
-
-    up_copies = {}
-
-    def rows_up():
-        for which in range(2):
-
-            def one(t, carry):
-                row_copy(which, t).wait_recv()
-                return carry
-
-            lax.fori_loop(1, COLS, one, 0)
-            for h, hop in enumerate(HOPS):
-                if (hop == 2) == (which == 1):
-                    up_copies[h] = remote(
-                        rows.at[place.half(which)], every.at[pl.ds(region(place.plane, 0), COLS)],
-                        up_s.at[h], up_r.at[h], place.above(hop),
-                    )
-                    up_copies[h].start()
-        every[pl.ds(region(place.plane, 0), COLS)] = rows[place.low]
-
-    def back_copy(h, t):
-        plane, col = place.up(CHUNKS[h]), place.turn(t)
+    def back_copy(slot, far, t):
+        plane, col = place.up(2 * far), place.turn(t)
         return remote(
-            step.at[1, lax.rem(plane, 2), col], every.at[region(place.plane, 1) + place.col],
-            back_s.at[h, t], back_r.at[h, t], place.at(place.core, plane, col),
+            step.at[slot, place.low, col], every.at[region(place.plane, slot) + place.col],
+            back_s.at[slot, far], back_r.at[slot, far], place.at(place.core, plane, col),
         )
 
-    def back_send():
+    def up_copy(slot, h, t):
+        col = place.turned(t)
+        return remote(
+            rows.at[slot, col], every.at[region(place.plane, slot) + col],
+            up_s.at[slot, h], up_r.at[slot, h], place.above(HOPS[h]),
+        )
+
+    def rows_send(slot):
+        def one(i, carry):
+            row_copy(slot, spread_order(i)).start()
+            return carry
+
+        lax.fori_loop(1, COLS, one, 0)
+        rows[slot, place.col] = step[slot, 1 - place.low, place.col]
+
+    def back_send(slot):
         def far(i, carry):
-            back_copy(2, spread_order(i)).start()
+            back_copy(slot, 1, spread_order(i)).start()
             return carry
 
-        def near(i, carry):
-            back_copy(0, spread_order(i)).start()
-            back_copy(1, spread_order(i)).start()
+        def here(i, carry):
+            back_copy(slot, 0, spread_order(i)).start()
             return carry
 
-        def here(i, carry):
-            back_copy(3, spread_order(i)).start()
+        lax.fori_loop(0, COLS, far, 0)
+        lax.fori_loop(1, COLS, here, 0)
+        every[region(place.plane, slot) + place.col] = step[slot, place.low, place.col]
+
+    def back_up(slot):
+        def up(t):
+            for h in range(2):
+                up_copy(slot, h, t).start()
+
+        def one(i, carry):
+            row_copy(slot, spread_order(i)).wait_recv()
+            up(spread_order(i))
             return carry
 
-        lax.fori_loop(0, COLS, far, 0)
-        lax.fori_loop(0, COLS, near, 0)
-        lax.fori_loop(1, COLS, here, 0)
-        every[region(place.plane, 1) + place.col] = step[1, place.low, place.col]
-
-    def back_wait(h):
-        def one(t, carry):
-            back_copy(h, t).wait_recv()
-            return carry
-
-        lax.fori_loop(int(CHUNKS[h] == 0), COLS, one, 0)
+        up(0)
+        lax.fori_loop(1, COLS, one, 0)
+
+    def piece(count):
+        return every.at[pl.ds(0, count)]
+
+    def row_all(slot):
+        return most(rows.at[slot, pl.ds(0, COLS - 1)], row_s.at[slot], row_r.at[slot, 0])
+
+    def back_all(slot, far):
+        return most(piece(COLS - 1 + far), back_s.at[slot, far], back_r.at[slot, far])
+
+    def up_all(slot, h):
+        return most(piece(COLS), up_s.at[slot, h], up_r.at[slot, h])
+
+    def back_over(slot):
+        for h in (3, 2, 0, 1):
+            if h < 2:
+                up_all(slot, h).wait_recv()
+            else:
+                back_all(slot, 3 - h).wait_recv()
+            over(slot, h)
+
+    def back_sent(slot):
+        row_all(slot).wait_send()
+        for h in range(2):
+            back_all(slot, h).wait_send()
+            up_all(slot, h).wait_send()
 
     back_cores = {}
 
@@ -405,72 +435,60 @@
         for side in range(2):
             gram[side, slot] = live[slot].astype(F32) * factor(side, slot, grad)
 
+    def sweep(with_result):
+        root_sweep(
+            [inverse.at[0], inverse.at[1]], [mixed.at[0], mixed.at[1]], [pair.at[0], pair.at[1]], with_result
+        )
+
     def sweeps(count):
         def one(i, carry):
-            root_sweep(inverse.at[0], mixed.at[0])
-            root_sweep(inverse.at[1], mixed.at[1])
+            sweep(True)
             return carry
 
         lax.fori_loop(0, count, one, 0)
 
+    for side in range(2):
+        for slot in range(CAP):
+            high, low = halves(keep[side, slot])
+            split[side, slot, 0:WIDTH] = high
+            split[side, slot, WIDTH : 2 * WIDTH] = low
     col_wait(AHEAD)
     for side in range(2):
-        root_start(factor(side, 0, grad_of(AHEAD)), inverse.at[side], mixed.at[side])
-    sweeps(1)
+        root_start(factor(side, 0, grad_of(AHEAD)), inverse.at[side], mixed.at[side], pair.at[side])
+    sweep(False)
+    sweep(True)
     col_wait(BEHIND)
-    put_step(0, kept_step(keep[0, 0], first_grad(), keep[1, 0]))
-    rows_send()
-    sweeps(1)
+    put_step(0, kept_step(split[0, 0], first_grad(), split[1, 0]))
+    rows_send(0)
     fold(SECOND, 0)
     fold(SECOND, 1)
+    back_send(0)
     sweeps(1)
-    rows_up()
+    back_up(0)
     sweeps(2)
     col_wait(SECOND)
-    put_step(1, kept_step(keep[0, 1], grad_of(SECOND), keep[1, 1]))
+    put_step(1, kept_step(split[0, 1], grad_of(SECOND), split[1, 1]))
     grad = grad_of(AHEAD)
-    inner = dot(inverse[0].astype(BF16), grad)
-    renewed = scaled_step(dot(inner.astype(BF16), inverse[1].astype(BF16)), grad)
+    root_left, root_right = [root_end(inverse.at[side], pair.at[side]).astype(BF16) for side in range(2)]
+    renewed = scaled_step(dot(dot(root_left, grad).astype(BF16), root_right), grad)
     late = step[1].reshape(WIDTH, WIDTH)
     put_step(1, jnp.where(fresh > 0, renewed.astype(F32), late.astype(F32)).astype(BF16))
-    back_send()
+    rows_send(1)
+    back_send(1)
+    back_up(1)
+    back_over(0)
     factors(0, first_grad())
     factors(1, grad_of(SECOND))
-    over(0, 3)
-    for h in range(len(HOPS)):
-        up_copies[h].wait_recv()
-        over(0, h)
     for h in range(PLANES):
         core_copies[SECOND, h].wait_send()
     for copy in plane_copies.values():
         copy.wait_send()
     for part in range(len(PARTS)):
         for which in range(2):
-
-            def done(t, carry):
-                col_copy(part, which, t).wait_send()
-                return carry
-
-            lax.fori_loop(1, COLS, done, 0)
-    for which in range(2):
-
-        def row_done(t, carry):
-            row_copy(which, t).wait_send()
-            return carry
-
-        lax.fori_loop(1, COLS, row_done, 0)
-    for copy in up_copies.values():
-        copy.wait_send()
-    for h in (2, 0, 1, 3):
-        back_wait(h)
-        over(1, h)
-    for h in range(len(CHUNKS)):
-
-        def back_done(t, carry):
-            back_copy(h, t).wait_send()
-            return carry
-
-        lax.fori_loop(int(CHUNKS[h] == 0), COLS, back_done, 0)
+            col_all(part, which).wait_send()
+    back_sent(0)
+    back_over(1)
+    back_sent(1)
     for copy in back_cores.values():
         copy.wait_recv()
 
@@ -519,8 +537,10 @@
             pltpu.SMEM((8, SLOTS), jnp.int32),
             pltpu.VMEM((count, ROWS, WIDTH), F32),
             pltpu.VMEM((2, CAP) + square, F32),
+            pltpu.VMEM((2, CAP, 2 * WIDTH, WIDTH), BF16),
             pltpu.VMEM((2,) + square, F32),
             pltpu.VMEM((2,) + square, F32),
+            pltpu.VMEM((2, 2 * WIDTH, WIDTH), BF16),
             pltpu.VMEM((PLANES,) + piece, F32),
             pltpu.VMEM((CAP, PLANES) + piece, F32),
             pltpu.VMEM((CAP, hops) + piece, BF16),
@@ -528,18 +548,18 @@
             pltpu.VMEM((CAP, 2) + piece, BF16),
             pltpu.VMEM((len(PARTS), 2) + piece, BF16),
             pltpu.VMEM((CAP, 2) + piece, BF16),
-            pltpu.VMEM((2,) + piece, BF16),
+            pltpu.VMEM((CAP,) + piece, BF16),
             pltpu.VMEM((SLOTS, ROWS, WIDTH), BF16),
             dma((9,)),
             dma((len(PARTS), PLANES)), dma((len(PARTS), PLANES)),
             dma((len(PARTS), hops)), dma((len(PARTS), hops)),
-            dma((len(PARTS), 2, COLS)), dma((len(PARTS), 2, COLS)),
-            dma((2, COLS)), dma((2, COLS)),
-            dma((hops,)), dma((hops,)),
-            dma((PLANES, COLS)), dma((PLANES, COLS)),
+            dma((len(PARTS), 2)), dma((len(PARTS), 2)),
+            dma((CAP,)), dma((CAP, COLS)),
+            dma((CAP, 2)), dma((CAP, 2)),
+            dma((CAP, 2)), dma((CAP, 2)),
             dma((CAP, PLANES)), dma((CAP, PLANES)),
         ],
-        compiler_params=pltpu.CompilerParams(collective_id=0, has_side_effects=True, vmem_limit_bytes=40 << 20),
+        compiler_params=pltpu.CompilerParams(collective_id=0, has_side_effects=True, vmem_limit_bytes=46 << 20),
     )(*[
         pltpu.with_memory_space_constraint(array, pltpu.HBM)
         for array in (

time: 77.6 us -> 72.4 us (0.933)
  Pallas kernels: 76.7 us -> 71.4 us
    pallas_call x1, Pallas kernels: 73.8 us -> 68.5 us  [body(): pl.pallas_call(whole_kernel, name='whole', out_shape=[pltpu.VMEM(params.s...]
where the time goes in v1:
time: 72.4 us; the launch traced here: 72.2 us
  Pallas kernels  71.4 us (99%)
  between operations  0.8 us (1%)
    pallas_call x1, Pallas kernels, body(): pl.pallas_call(whole_kernel, name='whole', out_shape=[pltpu.VMEM(params.s...  68.5 us
    pallas_call x1, Pallas kernels, body(): pl.pallas_call(store_kernel, name='store', out_shape=[jax.ShapeDtypeStruc...  2.9 us

profile of v1, /device:TPU:1, one launch (start us, length us, event | category | flops | bytes accessed | tf_op | source)
XLA Modules:
  0.0 72.2 jit_solution(12451124142009710980)
XLA Ops:
  0.6 68.5 %whole.1 = (bf16[160,16,512]{2,1,0:T(8,128)(2,1)S(1)}, f32[2,2,512,512]{3,2,1,0:T(8,128)S(1)}) custom-call(s32[1,160]{1,0:T(1,128)} %bitcast.2, s32[1,160]{1,0:T(1,128)} %bitcast.3, f32[1,160,16,512]{3,2,1,0:T(8,128)} %grad_hbm.1, bf16[160,16,512]{2,1,0:T(8,128)(2,1)} %params_hbm.1, f32[2,512,512]{2,1,0:T(8,128)} %stats_left.1, f32[2,512,512]{2,1,0:T(8,128)} %stats_right.1, ...), custom_call_target="tpu_custom_call" | custom-call | tf_op jit(solution)/shard_map/whole/pallas_call | solution.py:527
  69.1 2.9 %store.1 = (bf16[160,16,512]{2,1,0:T(8,128)(2,1)}, f32[2,512,512]{2,1,0:T(8,128)}, f32[2,512,512]{2,1,0:T(8,128)}) custom-call(bf16[160,16,512]{2,1,0:T(8,128)(2,1)S(1)} %get-tuple-element.5.result_ref, f32[2,2,512,512]{3,2,1,0:T(8,128)S(1)} %get-tuple-element.6.gram), custom_call_target="tpu_custom_call" | custom-call | tf_op jit(solution)/shard_map/store/pallas_call | solution.py:570

commit v2 on v1

--- a/solution.py
+++ b/solution.py
@@ -215,13 +215,24 @@
     core_copies = {}
     plane_copies = {}
 
+    def most(ref, send, recv):
+        return remote(ref, ref, send, recv, place.sibling())
+
+    def core_sent(part):
+        _, at, size, _ = PARTS[part]
+        most(core_out.at[:, pl.ds(at, size)], core_s.at[part], core_r.at[part, 0]).wait_send()
+
+    def plane_sent(part):
+        slot, at, size, _ = PARTS[part]
+        most(plane_out.at[slot, :, pl.ds(at, size)], plane_s.at[part], plane_r.at[part, 0]).wait_send()
+
     def pack(part):
         slot, at, size, _ = PARTS[part]
         for h, hop in enumerate(CHUNKS):
             start = base(1 - place.core, hop, part)
-            if part == SECOND:
-                core_copies[AHEAD, h].wait_send()
-                core_copies[BEHIND, h].wait_send()
+            if part == SECOND and h == 0:
+                core_sent(AHEAD)
+                core_sent(BEHIND)
 
             def one(e, carry, h=h, start=start):
                 core_out[h, at + e] = grad_ref[table[0, start + e]]
@@ -230,7 +241,7 @@
             lax.fori_loop(0, size, one, 0, unroll=4)
             span = pl.ds(at, size)
             core_copies[part, h] = remote(
-                core_out.at[h, span], core_in.at[slot, h, span], core_s.at[part, h], core_r.at[part, h], place.sibling()
+                core_out.at[h, span], core_in.at[slot, h, span], core_s.at[part], core_r.at[part, h], place.sibling()
             )
             core_copies[part, h].start()
 
@@ -252,7 +263,7 @@
             if hop:
                 span = pl.ds(at, size)
                 plane_copies[part, h] = remote(
-                    plane_out.at[slot, h, span], plane_in.at[slot, h, span], plane_s.at[part, h], plane_r.at[part, h],
+                    plane_out.at[slot, h, span], plane_in.at[slot, h, span], plane_s.at[part], plane_r.at[part, h],
                     place.above(hop),
                 )
                 if part != SECOND:
@@ -270,9 +281,6 @@
             col_s.at[part, which], col_r.at[part, which], place.at(place.core, place.plane, col),
         )
 
-    def most(ref, send, recv):
-        return remote(ref, ref, send, recv, place.sibling())
-
     def col_all(part, which):
         return most(held.at[part, place.half(which), pl.ds(0, COLS - 1)], col_s.at[part, which], col_r.at[part, which])
 
@@ -318,14 +326,14 @@
         plane, col = place.up(2 * far), place.turn(t)
         return remote(
             step.at[slot, place.low, col], every.at[region(place.plane, slot) + place.col],
-            back_s.at[slot, far], back_r.at[slot, far], place.at(place.core, plane, col),
+            back_s.at[slot], back_r.at[slot, far], place.at(place.core, plane, col),
         )
 
     def up_copy(slot, h, t):
         col = place.turned(t)
         return remote(
             rows.at[slot, col], every.at[region(place.plane, slot) + col],
-            up_s.at[slot, h], up_r.at[slot, h], place.above(HOPS[h]),
+            up_s.at[slot], up_r.at[slot, h], place.above(HOPS[h]),
         )
 
     def rows_send(slot):
@@ -369,10 +377,10 @@
         return most(rows.at[slot, pl.ds(0, COLS - 1)], row_s.at[slot], row_r.at[slot, 0])
 
     def back_all(slot, far):
-        return most(piece(COLS - 1 + far), back_s.at[slot, far], back_r.at[slot, far])
+        return most(piece(COLS - 1 + far), back_s.at[slot], back_r.at[slot, far])
 
     def up_all(slot, h):
-        return most(piece(COLS), up_s.at[slot, h], up_r.at[slot, h])
+        return most(piece(COLS), up_s.at[slot], up_r.at[slot, h])
 
     def back_over(slot):
         for h in (3, 2, 0, 1):
@@ -384,23 +392,21 @@
 
     def back_sent(slot):
         row_all(slot).wait_send()
-        for h in range(2):
-            back_all(slot, h).wait_send()
-            up_all(slot, h).wait_send()
-
-    back_cores = {}
+        most(piece(2 * COLS - 1), back_s.at[slot], back_r.at[slot, 0]).wait_send()
+        most(piece(2 * COLS), up_s.at[slot], up_r.at[slot, 0]).wait_send()
+
+    core_all = most(piece(SLOTS // 2), core_s2.at[0], core_r2.at[0])
 
     def over(slot, h):
         here = every.at[pl.ds(region(place.up(PLANES - CHUNKS[h]), slot), COLS)]
-        back_cores[slot, h] = remote(here, here, core_s2.at[slot, h], core_r2.at[slot, h], place.sibling())
-        back_cores[slot, h].start()
+        remote(here, here, core_s2.at[0], core_r2.at[0], place.sibling()).start()
 
     pack(AHEAD)
     pack(BEHIND)
     add(AHEAD)
     loads = []
     for i, (src, dst) in enumerate(
-        ((stats_left, gram.at[0]), (stats_right, gram.at[1]), (roots_left, keep.at[0]), (roots_right, keep.at[1]),
+        ((roots_left, keep.at[0]), (roots_right, keep.at[1]), (stats_left, gram.at[0]), (stats_right, gram.at[1]),
          (params_hbm, result_ref))
     ):
         copy = pltpu.make_async_copy(src, dst, local_sems.at[1 + i])
@@ -408,13 +414,20 @@
         loads.append(copy)
     add(BEHIND)
     pack(SECOND)
+    for copy in loads[:2]:
+        copy.wait()
+    for side in range(2):
+        for slot in range(CAP):
+            high, low = halves(keep[side, slot])
+            split[side, slot, 0:WIDTH] = high
+            split[side, slot, WIDTH : 2 * WIDTH] = low
     fold(AHEAD, 0)
     fold(AHEAD, 1)
     add(SECOND)
     fold(BEHIND, 0)
     planes_send(SECOND)
     fold(BEHIND, 1)
-    for copy in loads:
+    for copy in loads[2:]:
         copy.wait()
 
     def grad_of(part):
@@ -447,11 +460,6 @@
 
         lax.fori_loop(0, count, one, 0)
 
-    for side in range(2):
-        for slot in range(CAP):
-            high, low = halves(keep[side, slot])
-            split[side, slot, 0:WIDTH] = high
-            split[side, slot, WIDTH : 2 * WIDTH] = low
     col_wait(AHEAD)
     for side in range(2):
         root_start(factor(side, 0, grad_of(AHEAD)), inverse.at[side], mixed.at[side], pair.at[side])
@@ -479,18 +487,16 @@
     back_over(0)
     factors(0, first_grad())
     factors(1, grad_of(SECOND))
-    for h in range(PLANES):
-        core_copies[SECOND, h].wait_send()
-    for copy in plane_copies.values():
-        copy.wait_send()
+    core_sent(SECOND)
+    for part in range(len(PARTS)):
+        plane_sent(part)
     for part in range(len(PARTS)):
         for which in range(2):
             col_all(part, which).wait_send()
     back_sent(0)
     back_over(1)
     back_sent(1)
-    for copy in back_cores.values():
-        copy.wait_recv()
+    core_all.wait_recv()
 
     def apply(b, carry):
         change = every[table[1, b]].astype(F32)
@@ -498,16 +504,19 @@
         return carry
 
     lax.fori_loop(0, result_ref.shape[0], apply, 0, unroll=4)
-    for copy in back_cores.values():
-        copy.wait_send()
+    core_all.wait_send()
 
 
 def store_kernel(result_ref, gram, out_params, out_left, out_right, sems):
-    copies = [
-        pltpu.make_async_copy(gram.at[0], out_left, sems.at[0]),
-        pltpu.make_async_copy(gram.at[1], out_right, sems.at[1]),
-        pltpu.make_async_copy(result_ref, out_params, sems.at[2]),
-    ]
+    copies = []
+    for slot in range(CAP):
+        copies.append((gram.at[0, slot], out_left.at[slot]))
+        copies.append((gram.at[1, slot], out_right.at[slot]))
+    half = result_ref.shape[0] // 2
+    for part in range(2):
+        span = pl.ds(part * half, half)
+        copies.append((result_ref.at[span], out_params.at[span]))
+    copies = [pltpu.make_async_copy(src, dst, sems.at[i]) for i, (src, dst) in enumerate(copies)]
     for copy in copies:
         copy.start()
     for copy in copies:
@@ -551,13 +560,13 @@
             pltpu.VMEM((CAP,) + piece, BF16),
             pltpu.VMEM((SLOTS, ROWS, WIDTH), BF16),
             dma((9,)),
-            dma((len(PARTS), PLANES)), dma((len(PARTS), PLANES)),
-            dma((len(PARTS), hops)), dma((len(PARTS), hops)),
+            dma((len(PARTS),)), dma((len(PARTS), PLANES)),
+            dma((len(PARTS),)), dma((len(PARTS), hops)),
             dma((len(PARTS), 2)), dma((len(PARTS), 2)),
             dma((CAP,)), dma((CAP, COLS)),
-            dma((CAP, 2)), dma((CAP, 2)),
-            dma((CAP, 2)), dma((CAP, 2)),
-            dma((CAP, PLANES)), dma((CAP, PLANES)),
+            dma((CAP,)), dma((CAP, 2)),
+            dma((CAP,)), dma((CAP, 2)),
+            dma((1,)), dma((1,)),
         ],
         compiler_params=pltpu.CompilerParams(collective_id=0, has_side_effects=True, vmem_limit_bytes=46 << 20),
     )(*[
@@ -577,7 +586,7 @@
         ],
         in_specs=[VMEM] * 2,
         out_specs=[HBM] * 3,
-        scratch_shapes=[dma((3,))],
+        scratch_shapes=[dma((6,))],
         compiler_params=pltpu.CompilerParams(vmem_limit_bytes=1 << 20),
     )(
         pltpu.with_memory_space_constraint(result, pltpu.VMEM),

time: 72.4 us -> 72 us (level)
  no operation moved by 1% of the time
where the time goes in v2:
time: 72 us; the launch traced here: 71.8 us
  Pallas kernels  71 us (99%)
  between operations  0.8 us (1%)
    pallas_call x1, Pallas kernels, body(): pl.pallas_call(whole_kernel, name='whole', out_shape=[pltpu.VMEM(params.s...  68.1 us
    pallas_call x1, Pallas kernels, body(): pl.pallas_call(store_kernel, name='store', out_shape=[jax.ShapeDtypeStruc...  2.89 us

profile of v2, /device:TPU:1, one launch (start us, length us, event | category | flops | bytes accessed | tf_op | source)
XLA Modules:
  0.0 71.8 jit_solution(1082833951892442868)
XLA Ops:
  0.6 68.1 %whole.1 = (bf16[160,16,512]{2,1,0:T(8,128)(2,1)S(1)}, f32[2,2,512,512]{3,2,1,0:T(8,128)S(1)}) custom-call(s32[1,160]{1,0:T(1,128)} %bitcast.2, s32[1,160]{1,0:T(1,128)} %bitcast.3, f32[1,160,16,512]{3,2,1,0:T(8,128)} %grad_hbm.1, bf16[160,16,512]{2,1,0:T(8,128)(2,1)} %params_hbm.1, f32[2,512,512]{2,1,0:T(8,128)} %stats_left.1, f32[2,512,512]{2,1,0:T(8,128)} %stats_right.1, ...), custom_call_target="tpu_custom_call" | custom-call | tf_op jit(solution)/shard_map/whole/pallas_call | solution.py:536
  68.8 2.9 %store.1 = (bf16[160,16,512]{2,1,0:T(8,128)(2,1)}, f32[2,512,512]{2,1,0:T(8,128)}, f32[2,512,512]{2,1,0:T(8,128)}) custom-call(bf16[160,16,512]{2,1,0:T(8,128)(2,1)S(1)} %get-tuple-element.5.result_ref, f32[2,2,512,512]{3,2,1,0:T(8,128)S(1)} %get-tuple-element.6.gram), custom_call_target="tpu_custom_call" | custom-call | tf_op jit(solution)/shard_map/store/pallas_call | solution.py:579

commit v3 on v2

--- a/solution.py
+++ b/solution.py
@@ -344,7 +344,7 @@
         lax.fori_loop(1, COLS, one, 0)
         rows[slot, place.col] = step[slot, 1 - place.low, place.col]
 
-    def back_send(slot):
+    def back_send(slot, to_far=True, to_here=True):
         def far(i, carry):
             back_copy(slot, 1, spread_order(i)).start()
             return carry
@@ -353,7 +353,10 @@
             back_copy(slot, 0, spread_order(i)).start()
             return carry
 
-        lax.fori_loop(0, COLS, far, 0)
+        if to_far:
+            lax.fori_loop(0, COLS, far, 0)
+        if not to_here:
+            return
         lax.fori_loop(1, COLS, here, 0)
         every[region(place.plane, slot) + place.col] = step[slot, place.low, place.col]
 
@@ -482,8 +485,9 @@
     late = step[1].reshape(WIDTH, WIDTH)
     put_step(1, jnp.where(fresh > 0, renewed.astype(F32), late.astype(F32)).astype(BF16))
     rows_send(1)
-    back_send(1)
+    back_send(1, to_here=False)
     back_up(1)
+    back_send(1, to_far=False)
     back_over(0)
     factors(0, first_grad())
     factors(1, grad_of(SECOND))

time: 72 us -> 72.9 us (1.013)
  Pallas kernels: 71 us -> 72 us
    pallas_call x1, Pallas kernels: 68.1 us -> 69.1 us  [body(): pl.pallas_call(whole_kernel, name='whole', out_shape=[pltpu.VMEM(params.s...]
where the time goes in v3:
time: 72.9 us; the launch traced here: 72.8 us
  Pallas kernels  72 us (99%)
  between operations  0.8 us (1%)
    pallas_call x1, Pallas kernels, body(): pl.pallas_call(whole_kernel, name='whole', out_shape=[pltpu.VMEM(params.s...  69.1 us
    pallas_call x1, Pallas kernels, body(): pl.pallas_call(store_kernel, name='store', out_shape=[jax.ShapeDtypeStruc...  2.89 us

profile of v3, /device:TPU:1, one launch (start us, length us, event | category | flops | bytes accessed | tf_op | source)
XLA Modules:
  0.0 72.8 jit_solution(3256429489098011511)
XLA Ops:
  0.6 69.1 %whole.1 = (bf16[160,16,512]{2,1,0:T(8,128)(2,1)S(1)}, f32[2,2,512,512]{3,2,1,0:T(8,128)S(1)}) custom-call(s32[1,160]{1,0:T(1,128)} %bitcast.2, s32[1,160]{1,0:T(1,128)} %bitcast.3, f32[1,160,16,512]{3,2,1,0:T(8,128)} %grad_hbm.1, bf16[160,16,512]{2,1,0:T(8,128)(2,1)} %params_hbm.1, f32[2,512,512]{2,1,0:T(8,128)} %stats_left.1, f32[2,512,512]{2,1,0:T(8,128)} %stats_right.1, ...), custom_call_target="tpu_custom_call" | custom-call | tf_op jit(solution)/shard_map/whole/pallas_call | solution.py:540
  69.8 2.9 %store.1 = (bf16[160,16,512]{2,1,0:T(8,128)(2,1)}, f32[2,512,512]{2,1,0:T(8,128)}, f32[2,512,512]{2,1,0:T(8,128)}) custom-call(bf16[160,16,512]{2,1,0:T(8,128)(2,1)S(1)} %get-tuple-element.5.result_ref, f32[2,2,512,512]{3,2,1,0:T(8,128)S(1)} %get-tuple-element.6.gram), custom_call_target="tpu_custom_call" | custom-call | tf_op jit(solution)/shard_map/store/pallas_call | solution.py:583
